TPU v7x, 32 devices: a whole 2x2x4 slice. The times are simulated.
32 devices in a mesh: groups: 2 (over x), ctx: 8 (over z, y), head: 2 (over core).
Axes of the slice: x: 2, y: 2, z: 4, core: 2. Of those that a mesh axis runs over, the one named last changes fastest.
Arguments:
- prefix_x: bfloat16 [2048, 4096], P(('groups', 'ctx'), 'head'), parts along dimension 0, may hold values from -6 to 6
- prefix_z: bfloat16 [2048, 4096], P(('groups', 'ctx'), 'head'), parts along dimension 0, may hold values from -6 to 6
- prefix_b: bfloat16 [2048, 1024], P(('groups', 'ctx'), 'head'), parts along dimension 0, may hold values from -0.59765625 to 0.59765625
- prefix_c: bfloat16 [2048, 1024], P(('groups', 'ctx'), 'head'), parts along dimension 0, may hold values from -0.59765625 to 0.59765625
- prefix_decay: float32 [64, 2048], P('head', ('groups', 'ctx')), parts along dimension 1, may hold values from -0.7 to 0
- crit_x: bfloat16 [2048, 4096], P(('groups', 'ctx'), 'head'), parts along dimension 0, may hold values from -6 to 6
- crit_z: bfloat16 [2048, 4096], P(('groups', 'ctx'), 'head'), parts along dimension 0, may hold values from -6 to 6
- crit_b: bfloat16 [2048, 1024], P(('groups', 'ctx'), 'head'), parts along dimension 0, may hold values from -0.59765625 to 0.59765625
- crit_c: bfloat16 [2048, 1024], P(('groups', 'ctx'), 'head'), parts along dimension 0, may hold values from -0.59765625 to 0.59765625
- crit_decay: float32 [64, 2048], P('head', ('groups', 'ctx')), parts along dimension 1, may hold values from -0.7 to 0
- skip_weight: float32 [64], P('head'), may hold values from 0.5 to 1.5
- norm_gain: float32 [4096], P('head'), may hold values from 0.5 to 1.5
- crit_lengths: int32 [16], P(('groups', 'ctx')), parts along dimension 0, may hold values from 1 to 128, 768 in all
- crit_queries: bfloat16 [2048, 4096], P(('groups', 'ctx'), 'head'), parts along dimension 0, may hold values from -6 to 6
- crit_keys: bfloat16 [2048, 512], P(('groups', 'ctx'), 'head'), parts along dimension 0, may hold values from -6 to 6
- crit_values: bfloat16 [2048, 512], P(('groups', 'ctx'), 'head'), parts along dimension 0, may hold values from -6 to 6
- prefix_keys: bfloat16 [2048, 512], P(('groups', 'ctx'), 'head'), parts along dimension 0, may hold values from -6 to 6
- prefix_values: bfloat16 [2048, 512], P(('groups', 'ctx'), 'head'), parts along dimension 0, may hold values from -6 to 6
Outputs:
- prefix_mixed: bfloat16 [2048, 4096], P(('groups', 'ctx'), 'head'), parts along dimension 0
- crit_mixed: bfloat16 [2048, 4096], P(('groups', 'ctx'), 'head'), parts along dimension 0
- attended: bfloat16 [2048, 4096], P(('groups', 'ctx'), 'head'), parts along dimension 0
There are 2 independent parts, one for each index of `groups`. A program takes and returns all parts, laid end to end along the dimension named above; an argument that names none is the same for every part. Nothing has to cross between parts.
Inputs may be any that keep to these rules, and one draw needn't show every extreme that they name: Critique c holds crit_lengths[c] real tokens from slot c * 128 on; the rest of its slots are padding.
All inputs are finite; a program needn't handle non-finite values. No bound on the sum of `crit_lengths` on one device may be relied on, other than what follows from the above.
Results may differ from a plain program's by a relative error of at most 0.009.
Values may be sent and summed in bfloat16 or wider, within the bound.
A program may use at most 128 MiB of HBM per device.

v0:
```python
import jax
import jax.numpy as jnp
from jax import lax
from jax.sharding import PartitionSpec as P

NS = 128
DH = 128


norm_eps = 1e-05
key_block = 512


def prefix(array, axis, combine, identity):
    devices, position = (lax.axis_size(axis), lax.axis_index(axis))
    everything = jax.tree.map(
        lambda part, kind: lax.all_gather(part.astype(kind), axis),
        array,
        (jnp.bfloat16, jnp.bfloat16),
    )
    start = jax.tree.map(
        lambda part, zero: jnp.broadcast_to(jnp.asarray(zero, part.dtype), part.shape),
        array,
        identity,
    )

    def prefix_hop(k, before):
        reached = k < position
        new = combine(
            before, jax.tree.map(lambda part, own: part[k].astype(own.dtype), everything, array)
        )
        return jax.tree.map(lambda a, b: jnp.where(reached, a, b), new, before)

    return lax.fori_loop(0, devices, prefix_hop, start)


def entering(array, axis, combine, identity):
    devices, position = (lax.axis_size(axis), lax.axis_index(axis))
    everything = lax.all_gather(array, axis)
    start = jnp.broadcast_to(jnp.asarray(identity, array.dtype), array.shape)

    def entering_hop(k, before):
        at = devices - 1 - k
        reached = at > position
        new = combine(before, everything[at])
        return jnp.where(reached, new, before)

    return lax.fori_loop(0, devices, entering_hop, start)


def link(previous_rows, later):
    return (
        previous_rows[0] + later[0],
        jnp.exp(later[0])[..., None, None] * previous_rows[1] + later[1],
    )


def block_pieces(x_rows, b_rows, c_rows, log_decay, groups, with_state):
    steps = x_rows.shape[0]
    heads = log_decay.shape[0]
    width = x_rows.shape[1] // heads
    per_group = heads // groups
    cumulative = jnp.cumsum(log_decay, axis=1)
    cum_group = cumulative.reshape(groups, per_group, steps)
    inputs = x_rows.reshape(steps, groups, per_group, width)
    b_group = b_rows.reshape(steps, groups, NS)
    c_group = c_rows.reshape(steps, groups, NS)
    inner = jnp.einsum("tgn,sgn->gts", c_group, b_group, preferred_element_type=jnp.float32)
    later = lax.broadcasted_iota(jnp.int32, (steps, steps), 0) >= lax.broadcasted_iota(
        jnp.int32, (steps, steps), 1
    )
    gap = cum_group[:, :, :, None] - cum_group[:, :, None, :]
    mixing = (jnp.where(later, jnp.exp(jnp.where(later, gap, 0.0)), 0.0) * inner[:, None]).astype(
        jnp.bfloat16
    )
    within = jnp.einsum("gkts,sgkp->tgkp", mixing, inputs, preferred_element_type=jnp.float32)
    if not with_state:
        return (cumulative, within, None)
    tail = jnp.transpose(jnp.exp(cum_group[:, :, -1:] - cum_group), (2, 0, 1))[..., None]
    scaled = (inputs * tail).astype(jnp.bfloat16)
    local_state = jnp.einsum("sgkp,sgn->gkpn", scaled, b_group, preferred_element_type=jnp.float32)
    return (cumulative, within, local_state.reshape(heads, width, NS))


def finish(within, cumulative, entry, x_rows, c_rows, z_rows, skip_weight, norm_gain, groups):
    steps = x_rows.shape[0]
    heads = cumulative.shape[0]
    per_group = heads // groups
    width = x_rows.shape[1] // heads
    c_group = c_rows.reshape(steps, groups, NS).astype(jnp.float32)
    across = jnp.einsum(
        "tgn,gkpn->tgkp",
        c_group,
        entry.reshape(groups, per_group, width, NS),
        precision=lax.Precision.HIGHEST,
    )
    growth = jnp.transpose(jnp.exp(cumulative.reshape(groups, per_group, steps)), (2, 0, 1))[
        ..., None
    ]
    inputs = x_rows.reshape(steps, groups, per_group, width).astype(jnp.float32)
    output_rows = within + across * growth + skip_weight.reshape(groups, per_group, 1) * inputs
    gated = output_rows * jax.nn.silu(
        z_rows.reshape(steps, groups, per_group, width).astype(jnp.float32)
    )
    power = jnp.mean(gated * gated, axis=(2, 3), keepdims=True)
    normed = gated * lax.rsqrt(power + norm_eps) * norm_gain.reshape(groups, per_group, width)
    return normed.reshape(steps, heads * width)


def shards(
    prefix_x,
    prefix_z,
    prefix_b,
    prefix_c,
    prefix_decay,
    crit_x,
    crit_z,
    crit_b,
    crit_c,
    crit_decay,
    skip_weight,
    norm_gain,
    crit_lengths,
    crit_queries,
    crit_keys,
    crit_values,
    prefix_keys,
    prefix_values,
):
    groups = prefix_b.shape[1] // NS
    cumulative, within, local_state = block_pieces(
        prefix_x, prefix_b, prefix_c, prefix_decay, groups, True
    )
    total = cumulative[:, -1]
    identity = (jnp.zeros_like(total), jnp.zeros_like(local_state))
    scanned = prefix((total, local_state), "ctx", link, identity)
    entry = scanned[1]
    later_decay = entering(total, "ctx", jnp.add, jnp.zeros_like(total))
    final_state = lax.psum(jnp.exp(later_decay)[:, None, None] * local_state, "ctx")
    prefix_mixed = finish(
        within, cumulative, entry, prefix_x, prefix_c, prefix_z, skip_weight, norm_gain, groups
    )
    crit_cum, crit_within, unused = block_pieces(crit_x, crit_b, crit_c, crit_decay, groups, False)
    crit_mixed = finish(
        crit_within, crit_cum, final_state, crit_x, crit_c, crit_z, skip_weight, norm_gain, groups
    )
    rows = crit_x.shape[0]
    positions = lax.broadcasted_iota(jnp.int32, (rows, 1), 0)
    length = crit_lengths[0]
    crit_mixed = jnp.where(positions < length, crit_mixed, 0.0)
    kv_heads = crit_keys.shape[1] // DH
    ratio = crit_queries.shape[1] // (DH * kv_heads)
    scale = DH ** (-0.5)
    query_groups = crit_queries.reshape(rows, kv_heads, ratio, DH)
    own_keys = crit_keys.reshape(rows, kv_heads, DH)
    own_values = crit_values.reshape(rows, kv_heads, DH)
    scores = (
        jnp.einsum("qgrd,kgd->qgrk", query_groups, own_keys, preferred_element_type=jnp.float32)
        * scale
    )
    causal = lax.broadcasted_iota(jnp.int32, (rows, rows), 0) >= lax.broadcasted_iota(
        jnp.int32, (rows, rows), 1
    )
    scores = jnp.where(causal[:, None, None, :], scores, -jnp.inf)
    highest = jnp.max(scores, axis=-1)
    weights = jnp.exp(scores - highest[..., None])
    mass = jnp.sum(weights, axis=-1)
    summed = jnp.einsum(
        "qgrk,kgd->qgrd",
        weights.astype(jnp.bfloat16),
        own_values,
        preferred_element_type=jnp.float32,
    )
    piece = (
        lax.all_gather(prefix_keys, "ctx", axis=0, tiled=True),
        lax.all_gather(prefix_values, "ctx", axis=0, tiled=True),
    )
    count = piece[0].shape[0]
    key_blocks = piece[0].reshape(count // key_block, key_block, kv_heads, DH)
    value_blocks = piece[1].reshape(count // key_block, key_block, kv_heads, DH)

    def visit(state, block):
        best, weight_total, accum = state
        block_scores = (
            jnp.einsum("qgrd,kgd->qgrk", query_groups, block[0], preferred_element_type=jnp.float32)
            * scale
        )
        newest = jnp.maximum(best, jnp.max(block_scores, axis=-1))
        block_weights = jnp.exp(block_scores - newest[..., None])
        fade = jnp.exp(best - newest)
        weight_total = weight_total * fade + jnp.sum(block_weights, axis=-1)
        accum = accum * fade[..., None] + jnp.einsum(
            "qgrk,kgd->qgrd",
            block_weights.astype(jnp.bfloat16),
            block[1],
            preferred_element_type=jnp.float32,
        )
        return ((newest, weight_total, accum), None)

    highest, mass, summed = lax.scan(visit, (highest, mass, summed), (key_blocks, value_blocks))[0]
    attended = (summed / mass[..., None]).reshape(rows, ratio * kv_heads * DH)
    attended = jnp.where(positions < length, attended, 0.0)
    return (
        prefix_mixed.astype(jnp.bfloat16),
        crit_mixed.astype(jnp.bfloat16),
        attended.astype(jnp.bfloat16),
    )


def solution(mesh):
    in_specs = (
        P(("groups", "ctx"), "head"),
        P(("groups", "ctx"), "head"),
        P(("groups", "ctx"), "head"),
        P(("groups", "ctx"), "head"),
        P("head", ("groups", "ctx")),
        P(("groups", "ctx"), "head"),
        P(("groups", "ctx"), "head"),
        P(("groups", "ctx"), "head"),
        P(("groups", "ctx"), "head"),
        P("head", ("groups", "ctx")),
        P("head"),
        P("head"),
        P(("groups", "ctx")),
        P(("groups", "ctx"), "head"),
        P(("groups", "ctx"), "head"),
        P(("groups", "ctx"), "head"),
        P(("groups", "ctx"), "head"),
        P(("groups", "ctx"), "head"),
    )
    out_specs = (
        P(("groups", "ctx"), "head"),
        P(("groups", "ctx"), "head"),
        P(("groups", "ctx"), "head"),
    )
    return jax.shard_map(shards, mesh=mesh, in_specs=in_specs, out_specs=out_specs, check_vma=False)
```

profile of v0, /device:TPU:0, one launch (start us, length us, event | category | flops | bytes accessed | tf_op | source)
XLA Modules:
  0.0 220.7 jit_solution(5487582836714977756)
XLA Ops:
  7.2 1.0 reduce_window_sum.19
  9.5 1.3 copy.64
  10.8 1.1 reshape.148
  11.9 1.2 dynamic-slice
  14.0 23.1 %all-reduce.1 = f32[256]{0:T(256)S(1)} all-reduce(f32[256]{0:T(256)S(1)} %dynamic-update-slice.1), channel_id=2, replica_groups=mesh['groups'=2,'ctx'=8,'head'=2] {'ctx'}, use_global_device_ids=true, to_apply=%add.1 | all-reduce | flops 256 | bytes 2048
  37.6 1.1 fusion.63
  38.7 1.1 bitcast_multiply_fusion
  39.9 0.7 all-gather.4.cloned.1.call-update
  40.6 0.7 copy.61
  41.3 1.0 copy.71
  42.3 2.0 reduce_window_sum.21
  44.4 0.7 mul.169
  45.1 1.2 copy.73
  46.3 0.7 reshape.151
  46.9 0.7 mul.177
  48.6 1.0 copy-done.2
  49.5 1.4 convolution_bitcast_fusion
  50.9 1.6 copy.80
  52.5 31.9 %all_gather.20 = bf16[1024,256]{1,0:T(8,128)(2,1)S(1)} all-gather(bf16[128,256]{1,0:T(8,128)(2,1)S(1)} %copy-done.20), channel_id=1, replica_groups=mesh['groups'=2,'ctx'=8,'head'=2] {'ctx'}, dimensions={0}, use_global_device_ids=true | all-gather | bytes 589824 | tf_op jit(solution)/shard_map/all_gather | solution.py:175
  84.4 0.9 reshape.160
  85.3 32.1 %all_gather.21 = bf16[1024,256]{1,0:T(8,128)(2,1)S(1)} all-gather(bf16[128,256]{1,0:T(8,128)(2,1)S(1)} %copy-done.21), channel_id=1, replica_groups=mesh['groups'=2,'ctx'=8,'head'=2] {'ctx'}, dimensions={0}, use_global_device_ids=true | all-gather | bytes 589824 | tf_op jit(solution)/shard_map/all_gather | solution.py:176
  117.4 0.9 reshape.161
  118.4 1.4 fusion.39
  119.8 15.4 %while.44 = (s32[]{:T(128)}, f32[128,2,8]{0,2,1:T(8,128)S(1)}, f32[128,2,8]{0,2,1:T(8,128)S(1)}, f32[128,2,8,128]{0,3,2,1:T(8,128)S(1)}, bf16[2,512,2,128]{3,2,1...) while((s32[]{:T(128)}, f32[128,2,8]{0,2,1:T(8,128)S(1)}, ...), condition=%wide.region_14.15_spmd, body=%wide.region_11.14_spmd.sunk | while | flops 545787904 | bytes 34209908 | solution.py:200
  119.8 1.4 constant_dynamic-slice_fusion.3
  121.2 0.7 bitcast_reduce_fusion.2
  121.9 0.7 fusion.84
  122.6 1.2 copy-done.1
  124.0 3.4 %fusion.85 = f32[128,2,8,128]{0,3,2,1:T(8,128)S(1)} fusion(f32[2,512,128,8]{2,1,3,0:T(8,128)} %copy-done.1, f32[128,2,8]{0,2,1:T(8,128)S(1)} %max.4, f32[128,2,8,128]{0,3,2,1:T(8,128)S(1)} %get-tuple-element.505, f32[128,2,8]{0,2,1:T(8,128)S(1)} %get-tuple-element.462, bf16[1,512,2,128]{1,3,2,0:T(8,128)(2,1)S(1)} %copy.155), kind=kOutput, calls=%fused_computation.9.clone.1 | convolution fusion | flops 272105472 | bytes 6569984 | tf_op jit(solution)/shard_map/while/body/eval_jaxpr/qgrk,kgd->qgrd/dot_general | solution.py:192
  127.4 1.4 constant_dynamic-slice_fusion.3
  128.9 0.7 bitcast_reduce_fusion.2
  129.6 0.7 fusion.84
  130.3 1.2 copy-done.1
  131.7 3.3 %fusion.85 = f32[128,2,8,128]{0,3,2,1:T(8,128)S(1)} fusion(f32[2,512,128,8]{2,1,3,0:T(8,128)} %copy-done.1, f32[128,2,8]{0,2,1:T(8,128)S(1)} %max.4, f32[128,2,8,128]{0,3,2,1:T(8,128)S(1)} %get-tuple-element.505, f32[128,2,8]{0,2,1:T(8,128)S(1)} %get-tuple-element.462, bf16[1,512,2,128]{1,3,2,0:T(8,128)(2,1)S(1)} %copy.155), kind=kOutput, calls=%fused_computation.9.clone.1 | convolution fusion | flops 272105472 | bytes 6569984 | tf_op jit(solution)/shard_map/while/body/eval_jaxpr/qgrk,kgd->qgrd/dot_general | solution.py:192
  136.2 0.9 fusion.60
  137.4 18.1 %all-reduce = bf16[256]{0:T(256)(128)(2,1)S(1)} all-reduce(bf16[256]{0:T(256)(128)(2,1)S(1)} %dynamic-update-slice), channel_id=3, replica_groups=mesh['groups'=2,'ctx'=8,'head'=2] {'ctx'}, use_global_device_ids=true, to_apply=%add | all-reduce | flops 256 | bytes 1024
  155.5 0.6 reshape.168
  156.1 2.2 %copy.68 = f32[128,2048]{0,1:T(8,128)} copy(bf16[128,2048]{1,0:T(8,128)(2,1)} %param.25) | data formatting | bytes 1572864 | tf_op jit(solution)/shard_map/convert_element_type | solution.py:103
  158.3 0.7 reshape.147
  159.5 0.6 exponential_bitcast_fusion.1
  160.6 1.9 convolution_bitcast_fusion.4
  162.6 1.9 convolution_bitcast_fusion.3
  164.5 2.7 %multiply_reduce_fusion = (f32[128,4]{0,1:T(4,128)S(1)}, f32[128,4,8,64]{0,3,2,1:T(8,128)S(1)}) fusion(f32[128,4,8,64]{0,3,2,1:T(8,128)S(1)} %bitcast.166, bf16[128,4,8,64]{0,3,2,1:T(8,128)(2,1)} %bitcast.169, f32[4,8]{1,0:T(4,128)S(1)} %copy-done.31, f32[128,4,8,64]{0,3,2,1:T(8,128)} %convolution_bitcast_fusion.3, f32[128,4,8]{0,2,1:T(8,128)S(1)} %copy-done.29, ...), kind=kOutput, calls=%fused_computation.49 | convolution fusion | flops 405798400 | bytes 4868224 | tf_op jit(solution)/shard_map/tgn,gkpn->tgkp/dot_general | solution.py:91
  167.8 1.3 select_convert_fusion
  169.1 25.5 %all-gather.4.cloned.1.call-done = bf16[8,32,64,128]{3,2,1,0:T(8,128)(2,1)} async-done(((bf16[1,32,64,128]{3,2,1,0:T(8,128)(2,1)}), bf16[8,32,64,128]{3,2,1,0:T(8,128)(2,1)}) %all-gather.4.cloned.1.call-update) | async-done | bytes 4194320 | tf_op jit(solution)/shard_map/all_gather | solution.py:17
  194.6 15.6 %while.45 = (s32[]{:T(128)}, f32[32,64,128]{2,1,0:T(8,128)S(1)}, s32[]{:T(128)}, bf16[8,32]{1,0:T(8,128)(2,1)}, bf16[8,32,64,128]{3,2,1,0:T(8,128)(2,1)}, /*index=5*/s32[]{:T(128)}, s32[]{:T(128)}) while((s32[]{:T(128)}, f32[32,64,128]{2,1,0:T(8,128)S(1)}, s32[]{:T(128)}, bf16[8,32]{1,0:T(8,128)(2,1)}, ...), condition=%wide.region_2.3_spmd.clone, body=%wide.region_1.2_spmd.clone.sunk | while | flops 1310756 | bytes 2621865 | solution.py:34
  194.6 0.7 exponential_bitcast_fusion.5
  195.3 1.3 fusion.86
  196.6 0.6 exponential_bitcast_fusion.5
  197.2 1.3 fusion.86
  198.6 0.6 exponential_bitcast_fusion.5
  199.2 1.3 fusion.86
  200.5 0.6 exponential_bitcast_fusion.5
  201.1 1.3 fusion.86
  202.5 0.6 exponential_bitcast_fusion.5
  203.1 1.3 fusion.86
  204.4 0.6 exponential_bitcast_fusion.5
  205.0 1.3 fusion.86
  206.3 0.6 exponential_bitcast_fusion.5
  207.0 1.3 fusion.86
  208.3 0.6 exponential_bitcast_fusion.5
  208.9 1.3 fusion.86
  210.3 2.2 %multiply_reduce_fusion.1 = (f32[128,4]{0,1:T(4,128)S(1)}, f32[128,4,8,64]{0,3,2,1:T(8,128)S(1)}) fusion(f32[128,4,8,64]{0,3,2,1:T(8,128)S(1)} %bitcast.167, bf16[128,4,8,64]{0,3,2,1:T(8,128)(2,1)S(1)} %bitcast.161, f32[4,8]{1,0:T(4,128)S(1)} %copy-done.31, f32[128,4,8,64]{0,3,2,1:T(8,128)} %convolution_bitcast_fusion.4, f32[128,4,8]{0,2,1:T(8,128)S(1)} %copy-done.25, ...), kind=kOutput, calls=%fused_computation.54 | convolution fusion | flops 405798400 | bytes 4868224 | tf_op jit(solution)/shard_map/tgn,gkpn->tgkp/dot_general | solution.py:91
  212.9 1.0 copy.85
  (116 shorter events, 5.9 us)
Async XLA Ops:
  7.2 153.2 %copy-start = (bf16[128,512]{1,0:T(8,128)(2,1)S(1)}, bf16[128,512]{1,0:T(8,128)(2,1)}, u32[]{:S(2)}) copy-start(bf16[128,512]{1,0:T(8,128)(2,1)} %param.31) | copy-start | bytes 393220
  7.2 157.3 %all-reduce.4.cloned.1.call-start = ((), (), s32[]{:S(2)}) async-start(), calls=%async_computation.1 | async-start | bytes 2097152 | tf_op jit(solution)/shard_map/psum | solution.py:139
  8.2 0.6 copy-start.15
  10.8 29.0 %copy-start.3 = (bf16[128,2048]{0,1:T(8,128)(2,1)}, bf16[128,2048]{0,1:T(8,128)(2,1)S(1)}, u32[]{:S(2)}) copy-start(bf16[128,2048]{0,1:T(8,128)(2,1)S(1)} %copy.64) | copy-start | bytes 1572868
  38.7 2.7 %copy-start.8 = (bf16[128,2048]{1,0:T(8,128)(2,1)S(1)}, bf16[128,2048]{1,0:T(8,128)(2,1)}, u32[]{:S(2)}) copy-start(bf16[128,2048]{1,0:T(8,128)(2,1)} %param.29) | copy-start | bytes 1572868
  38.7 3.7 %copy-start.26 = (f32[32,128]{1,0:T(8,128)S(1)}, f32[32,128]{1,0:T(8,128)}, u32[]{:S(2)}) copy-start(f32[32,128]{1,0:T(8,128)} %param.33) | copy-start | bytes 49156
  38.7 5.7 %copy-start.33 = (f32[32]{0:T(128)S(1)}, f32[32]{0:T(128)}, u32[]{:S(2)}) copy-start(f32[32]{0:T(128)} %param.34) | copy-start | bytes 388
  38.7 6.4 %copy-start.7 = (bf16[128,2048]{1,0:T(8,128)(2,1)S(1)}, bf16[128,2048]{1,0:T(8,128)(2,1)}, u32[]{:S(2)}) copy-start(bf16[128,2048]{1,0:T(8,128)(2,1)} %param.30) | copy-start | bytes 1572868
  39.8 6.5 %copy-start.13 = (bf16[128,512]{1,0:T(8,128)(2,1)S(1)}, bf16[128,512]{1,0:T(8,128)(2,1)}, u32[]{:S(2)}) copy-start(bf16[128,512]{1,0:T(8,128)(2,1)} %param.32) | copy-start | bytes 393220
  39.8 7.2 %copy-start.30 = (f32[2048]{0:T(1024)S(1)}, f32[2048]{0:T(1024)}, u32[]{:S(2)}) copy-start(f32[2048]{0:T(1024)} %param.35) | copy-start | bytes 24580
  39.8 7.8 %copy-start.9 = (bf16[128,2048]{1,0:T(8,128)(2,1)S(1)}, bf16[128,2048]{1,0:T(8,128)(2,1)}, u32[]{:S(2)}) copy-start(bf16[128,2048]{1,0:T(8,128)(2,1)} %param.37) | copy-start | bytes 1572868
  39.8 154.8 %all-gather.4.cloned.1.call-start = ((), (), s32[]{:S(2)}) async-start(), calls=%async_computation | async-start | bytes 4718592 | tf_op jit(solution)/shard_map/all_gather | solution.py:17
  40.6 7.3 %copy-start.22 = (bf16[128,256]{1,0:T(8,128)(2,1)S(1)}, bf16[128,256]{1,0:T(8,128)(2,1)}, u32[]{:S(2)}) copy-start(bf16[128,256]{1,0:T(8,128)(2,1)} %param.38) | copy-start | bytes 196612
  40.6 7.4 %copy-start.23 = (bf16[128,256]{1,0:T(8,128)(2,1)S(1)}, bf16[128,256]{1,0:T(8,128)(2,1)}, u32[]{:S(2)}) copy-start(bf16[128,256]{1,0:T(8,128)(2,1)} %param.39) | copy-start | bytes 196612
  48.5 1.0 copy-start.2
  49.5 3.0 %copy-start.20 = (bf16[128,256]{1,0:T(8,128)(2,1)S(1)}, bf16[128,256]{1,0:T(8,128)(2,1)}, u32[]{:S(2)}) copy-start(bf16[128,256]{1,0:T(8,128)(2,1)} %param.40) | copy-start | bytes 196612
  50.9 34.4 %copy-start.21 = (bf16[128,256]{1,0:T(8,128)(2,1)S(1)}, bf16[128,256]{1,0:T(8,128)(2,1)}, u32[]{:S(2)}) copy-start(bf16[128,256]{1,0:T(8,128)(2,1)} %param.41) | copy-start | bytes 196612
  121.9 2.0 copy-start.1
  129.6 2.0 copy-start.1
  135.1 23.2 %copy-start.12 = (bf16[128,512]{1,0:T(8,128)(2,1)S(1)}, bf16[128,512]{1,0:T(8,128)(2,1)}, u32[]{:S(2)}) copy-start(bf16[128,512]{1,0:T(8,128)(2,1)} %param.27) | copy-start | bytes 393220
  135.1 25.0 %copy-start.11 = (bf16[128,512]{1,0:T(8,128)(2,1)S(1)}, bf16[128,512]{1,0:T(8,128)(2,1)}, u32[]{:S(2)}) copy-start(bf16[128,512]{1,0:T(8,128)(2,1)} %param.26) | copy-start | bytes 393220
  135.3 24.2 %copy-start.24 = (f32[4,8,128]{2,1,0:T(8,128)S(1)}, f32[4,8,128]{2,1,0:T(8,128)}, u32[]{:S(2)}) copy-start(f32[4,8,128]{2,1,0:T(8,128)} %reduce_window_sum.21) | copy-start | bytes 49156
  135.3 25.1 %copy-start.14 = (bf16[128,512]{1,0:T(8,128)(2,1)S(1)}, bf16[128,512]{1,0:T(8,128)(2,1)}, u32[]{:S(2)}) copy-start(bf16[128,512]{1,0:T(8,128)(2,1)} %param.32) | copy-start | bytes 393220
  135.3 25.3 %copy-start.4 = (bf16[128,2048]{0,1:T(8,128)(2,1)S(1)}, bf16[128,2048]{0,1:T(8,128)(2,1)}, u32[]{:S(2)}) copy-start(bf16[128,2048]{0,1:T(8,128)(2,1)} %copy-done.3) | copy-start | bytes 1572868
  135.3 25.3 %copy-start.16 = (f32[32,128]{1,0:T(8,128)S(1)}, f32[32,128]{1,0:T(8,128)}, u32[]{:S(2)}) copy-start(f32[32,128]{1,0:T(8,128)} %copy-done.15) | copy-start | bytes 49156
  135.3 25.3 %copy-start.27 = (pred[128,128]{1,0:T(8,128)(4,1)S(1)}, pred[128,128]{1,0:T(8,128)(4,1)}, u32[]{:S(2)}) copy-start(pred[128,128]{1,0:T(8,128)(4,1)} %copy.61) | copy-start | bytes 49156
  160.6 1.9 copy-start.10
  160.6 1.9 copy-start.28
  162.5 1.9 copy-start.5
  162.5 1.9 copy-start.18
  162.5 1.9 copy-start.29
  162.6 1.9 copy-start.31
  164.5 2.8 %copy-start.17 = (f32[4,8,64]{2,1,0:T(8,128)S(1)}, f32[4,8,64]{2,1,0:T(8,128)}, u32[]{:S(2)}) copy-start(f32[4,8,64]{2,1,0:T(8,128)} %mul.177) | copy-start | bytes 24580
  167.2 0.6 copy-start.32
  194.6 15.7 %copy-start.6 = (f32[128,2048]{0,1:T(8,128)S(1)}, f32[128,2048]{0,1:T(8,128)}, u32[]{:S(2)}) copy-start(f32[128,2048]{0,1:T(8,128)} %copy.68) | copy-start | bytes 3145732
  194.6 15.7 %copy-start.19 = (bf16[128,4,128]{2,1,0:T(4,128)(2,1)S(1)}, bf16[128,4,128]{2,1,0:T(4,128)(2,1)}, u32[]{:S(2)}) copy-start(bf16[128,4,128]{2,1,0:T(4,128)(2,1)} %reshape.147) | copy-start | bytes 393220
  194.6 15.7 %copy-start.25 = (f32[128,4,8]{0,2,1:T(8,128)S(1)}, f32[128,4,8]{0,2,1:T(8,128)}, u32[]{:S(2)}) copy-start(f32[128,4,8]{0,2,1:T(8,128)} %get-tuple-element.350) | copy-start | bytes 49156
Sparse Core Ops, SparseCore 0:
  39.9 79.0 all-reduce.3
  121.9 72.6 all-gather.3
where the time goes:
time: 222 us; the launch traced here: 221 us
  blocking collectives  105 us (47%)
  local copies, waits for them, and re-layouts  27 us (12%)
  waiting for transfers between devices  26.2 us (12%)
  other arithmetic  25.8 us (12%)
  matrix products  20.1 us (9%)
  between operations  15.8 us (7%)
    unnamed x2, blocking collectives  41.2 us
    all_gather x1, blocking collectives, shards(): lax.all_gather(prefix_values, 'ctx', axis=0, tiled=True)  32.1 us
    all_gather x1, blocking collectives, shards(): lax.all_gather(prefix_keys, 'ctx', axis=0, tiled=True)  31.9 us
    all_gather x1, waiting for transfers between devices, prefix(): lax.all_gather(part.astype(kind), axis)  25.5 us
    select_n x8, other arithmetic, prefix_hop(): return jax.tree.map(lambda a, b: jnp.where(reached, a, b), new, before)  10.4 us
    unnamed x76, local copies, waits for them, and re-layouts  6.79 us
    dot_general x2, matrix products, visit(): jnp.einsum('qgrk,kgd->qgrd', block_weights.astype(jnp.bfloat16), block[1]...  6.69 us
    exp x8, other arithmetic, link(): jnp.exp(later[0])[..., None, None] * previous_rows[1] + later[1]  5.11 us
  transfers between devices with their start and end apart: 2, of which 1 were waited for; matrix products, arithmetic and copies ran while one was open for 19% of the time, Pallas kernels for 0%

commit v1 on v0

v1 whole, which is shorter than its diff:
```python
import functools
import math

import jax
import jax.numpy as jnp
from jax import lax
from jax.experimental import pallas as pl
from jax.experimental.pallas import tpu as pltpu
from jax.sharding import PartitionSpec as P

NS = 128
DH = 128
NORM_EPS = 1e-05
CHUNKS = 4
LOG2E = 1.4426950408889634
MESH = pl.DeviceIdType.MESH
HI = lax.Precision.HIGHEST
F32 = jnp.float32
BF16 = jnp.bfloat16


def nt(a, b, precision=None):
    return lax.dot_general(
        a, b, (((1,), (1,)), ((), ())), preferred_element_type=F32, precision=precision
    )


def nn(a, b, precision=None):
    return jnp.dot(a, b, preferred_element_type=F32, precision=precision)


def kernel(
    n,
    px,
    pz,
    pb,
    pc,
    pd,
    cx,
    cz,
    cb,
    cc,
    cd,
    skip,
    gain,
    length_ref,
    q_ref,
    ck,
    cv,
    pk,
    pv,
    out_p,
    out_c,
    out_a,
    kv,
    s_own,
    s_send,
    s_in,
    pair,
    e_out,
    e_in,
    r_out,
    r_in,
    x_out,
    state,
    e_keep,
    within_p,
    within_c,
    grow_p,
    grow_c,
    cols_p,
    cols_c,
    rows_p,
    rows_c,
    skips,
    kvy_s,
    kvy_r,
    up_s,
    up_r,
    dn_s,
    dn_r,
    s_s,
    s_r,
    e_s,
    e_r,
    r_s,
    r_r,
    x_s,
    x_r,
):
    me = lax.axis_index("ctx")
    y = lax.rem(me, 2)
    z = lax.div(me, 2)
    nz = n // 2
    other = me + 1 - 2 * y
    has_up = z < nz - 1
    has_dn = z > 0
    steps = px.shape[0]
    groups = pb.shape[1] // NS
    per = pd.shape[0] // groups
    gw = px.shape[1] // groups
    width = gw // per
    cw = s_own.shape[2]
    tail_rows = s_send.shape[1] - NS

    barrier = pltpu.get_barrier_semaphore()
    pl.semaphore_signal(barrier, inc=1, device_id={"ctx": other}, device_id_type=MESH)

    @pl.when(has_up)
    def _():
        pl.semaphore_signal(barrier, inc=1, device_id={"ctx": me + 2}, device_id_type=MESH)

    @pl.when(has_dn)
    def _():
        pl.semaphore_signal(barrier, inc=1, device_id={"ctx": me - 2}, device_id_type=MESH)

    def remote(src, dst, ss, rs, to):
        return pltpu.make_async_remote_copy(
            src_ref=src,
            dst_ref=dst,
            send_sem=ss,
            recv_sem=rs,
            device_id={"ctx": to},
            device_id_type=MESH,
        )

    kv_y = remote(kv.at[me], kv.at[me], kvy_s, kvy_r, other)
    s_c = [
        remote(
            s_send.at[(1 - y) * CHUNKS + c], s_in.at[c], s_s.at[c], s_r.at[c], other
        )
        for c in range(CHUNKS)
    ]
    e_c = [remote(e_out.at[c], e_in.at[c], e_s.at[c], e_r.at[c], me + 2) for c in range(CHUNKS)]
    r_c = [remote(r_out.at[c], r_in.at[c], r_s.at[c], r_r.at[c], me - 2) for c in range(CHUNKS)]
    x_c = [
        remote(x_out.at[c], state.at[y * CHUNKS + c], x_s.at[c], x_r.at[c], other)
        for c in range(CHUNKS)
    ]

    def kv_up(j):
        at = kv.at[pl.ds(2 * (z - j), 2)]
        return remote(at, at, up_s.at[j], up_r.at[j], me + 2)

    def kv_dn(j):
        at = kv.at[pl.ds(2 * (z + j), 2)]
        return remote(at, at, dn_s.at[j], dn_r.at[j], me - 2)

    def kv_send(j):
        @pl.when(jnp.logical_and(has_up, z - j >= 0))
        def _():
            kv_up(j).start()

        @pl.when(jnp.logical_and(has_dn, z + j < nz))
        def _():
            kv_dn(j).start()

    def kv_recv(j):
        @pl.when(z - 1 - j >= 0)
        def _():
            at = kv.at[pl.ds(2 * (z - 1 - j), 2)]
            remote(at, at, up_s.at[j], up_r.at[j], me + 2).wait_recv()

        @pl.when(z + 1 + j < nz)
        def _():
            at = kv.at[pl.ds(2 * (z + 1 + j), 2)]
            remote(at, at, dn_s.at[j], dn_r.at[j], me - 2).wait_recv()

    kv[me, 0] = pk[...]
    kv[me, 1] = pv[...]
    t_at = lax.broadcasted_iota(jnp.int32, (steps, steps), 0)
    s_at = lax.broadcasted_iota(jnp.int32, (steps, steps), 1)
    later = t_at >= s_at
    tri = jnp.where(later, 1.0, 0.0)
    spread = jnp.where(
        lax.broadcasted_iota(jnp.int32, (per, gw), 1) // width
        == lax.broadcasted_iota(jnp.int32, (per, gw), 0),
        1.0,
        0.0,
    )
    rows_p[...] = nt(pd[...], tri, HI)
    rows_c[...] = nt(cd[...], tri, HI)
    half_chunks = gw // cw
    for g in range(groups):
        col = nt(tri, pd[g * per : (g + 1) * per, :], HI)
        cols_p[g] = col
        cols_c[g] = nt(tri, cd[g * per : (g + 1) * per, :], HI)
        grow = nn(jnp.exp(col), spread, HI)
        grow_p[g] = grow
        tail = nn(jnp.exp(col[steps - 1 : steps, :] - col), spread, HI)
        lanes = slice(g * gw, (g + 1) * gw)
        scaled = (px[:, lanes].astype(F32) * tail).astype(BF16)
        b_t = pb[:, g * NS : (g + 1) * NS].astype(F32).T.astype(BF16)
        local = nn(b_t, scaled)
        low = local.astype(BF16)
        last = jnp.broadcast_to(grow[steps - 1 : steps, :], (8, gw))
        last_hi = last.astype(BF16)
        last_lo = (last - last_hi.astype(F32)).astype(BF16)
        code = jnp.concatenate([last_hi, last_lo], axis=0)
        for k in range(half_chunks):
            at = g * half_chunks + k
            s_own[at] = local[:, k * cw : (k + 1) * cw]
            s_send[at, 0:NS] = low[:, k * cw : (k + 1) * cw]
            s_send[at, NS : NS + tail_rows] = code[:, k * cw : (k + 1) * cw]
        skips[g] = nn(jnp.broadcast_to(skip[:, g * per : (g + 1) * per], (8, per)), spread, HI)

    peers = 1 + jnp.where(has_up, 1, 0) + jnp.where(has_dn, 1, 0)
    pl.semaphore_wait(barrier, peers)

    s_c[0].start()
    kv_y.start()
    for c in range(1, CHUNKS):
        s_c[c].start()

    lane = lax.broadcasted_iota(jnp.int32, (steps, 2 * width), 1)

    def within(x_ref, b_ref, c_ref, cols, rows, result):
        def group(g, carry):
            off = pl.multiple_of(g * NS, NS)
            inner = nt(c_ref[:, pl.ds(off, NS)], b_ref[:, pl.ds(off, NS)])
            col = cols[g]
            row = rows[pl.ds(pl.multiple_of(g * per, per), per), :]
            for k in range(per // 2):
                mixed = []
                for h in (2 * k, 2 * k + 1):
                    gap = col[:, h : h + 1] - row[h : h + 1, :]
                    mixed.append(
                        (jnp.exp(jnp.where(later, gap, -jnp.inf)) * inner).astype(BF16)
                    )
                xs = x_ref[:, pl.ds(pl.multiple_of(g * gw + k * 2 * width, NS), 2 * width)]
                zero = jnp.zeros_like(xs)
                both = jnp.concatenate(
                    [jnp.where(lane < width, xs, zero), jnp.where(lane < width, zero, xs)], axis=0
                )
                result[g, :, k * 2 * width : (k + 1) * 2 * width] = nn(
                    jnp.concatenate(mixed, axis=1), both
                )
            return carry

        lax.fori_loop(0, groups, group, 0)

    within(px, pb, pc, cols_p, rows_p, within_p)

    kv_y.wait_recv()
    kv_send(0)

    def decode(ref, c):
        return ref[c, NS : NS + 1].astype(F32) + ref[c, NS + 8 : NS + 9].astype(F32)

    def own_decay(c):
        at = y * CHUNKS + c
        return s_send[at, NS : NS + 1].astype(F32) + s_send[at, NS + 8 : NS + 9].astype(F32)

    def pair_decay(c):
        return own_decay(c) * decode(s_in, c)

    for c in range(CHUNKS):
        s_c[c].wait_recv()
        mine = s_own[y * CHUNKS + c]
        his = s_in[c, 0:NS].astype(F32)
        pair[c] = jnp.where(y == 0, his + decode(s_in, c) * mine, mine + own_decay(c) * his)

        @pl.when(jnp.logical_not(has_dn))
        def _():
            e_out[c] = pair[c].astype(BF16)
            e_keep[c] = jnp.zeros_like(e_keep[c])
            e_c[c].start()

        @pl.when(jnp.logical_not(has_up))
        def _():
            r_out[c, 0:NS] = pair[c].astype(BF16)
            code_decay(r_out, c, pair_decay(c))
            r_c[c].start()

    def chain_e(c):
        @pl.when(has_dn)
        def _():
            e_c[c].wait_recv()
            got = e_in[c].astype(F32)
            e_keep[c] = got

            @pl.when(has_up)
            def _():
                e_out[c] = (pair_decay(c) * got + pair[c]).astype(BF16)
                e_c[c].start()

    def chain_r(c):
        @pl.when(has_up)
        def _():
            r_c[c].wait_recv()

            @pl.when(has_dn)
            def _():
                after = decode(r_in, c)
                r_out[c, 0:NS] = (after * pair[c] + r_in[c, 0:NS].astype(F32)).astype(BF16)
                code_decay(r_out, c, after * pair_decay(c))
                r_c[c].start()

    def settle(c):
        at = y * CHUNKS + c
        entry = e_keep[c]
        through = pair_decay(c) * entry + pair[c]

        @pl.when(has_up)
        def _():
            x_out[c, 1] = (
                decode(r_in, c) * through + r_in[c, 0:NS].astype(F32)
            ).astype(BF16)

        @pl.when(jnp.logical_not(has_up))
        def _():
            x_out[c, 1] = through.astype(BF16)

        state[at, 1] = x_out[c, 1]
        first = entry.astype(BF16)

        @pl.when(y == 0)
        def _():
            state[at, 0] = first
            x_out[c, 0] = (own_decay(c) * entry + s_own[at]).astype(BF16)

        @pl.when(y != 0)
        def _():
            x_out[c, 0] = first
            state[at, 0] = (decode(s_in, c) * entry + s_in[c, 0:NS].astype(F32)).astype(BF16)

        x_c[c].start()

    low_half = 2 * z < nz

    @pl.when(low_half)
    def _():
        for c in range(CHUNKS):
            chain_e(c)

    @pl.when(jnp.logical_not(low_half))
    def _():
        for c in range(CHUNKS):
            chain_r(c)

    if nz > 1:
        kv_recv(0)
        if nz > 2:
            kv_send(1)

    @pl.when(low_half)
    def _():
        for c in range(CHUNKS):
            chain_r(c)

    @pl.when(jnp.logical_not(low_half))
    def _():
        for c in range(CHUNKS):
            chain_e(c)

    for c in range(CHUNKS):
        settle(c)

    for g in range(groups):
        grow_c[g] = nn(jnp.exp(cols_c[g]), spread, HI)
    within(cx, cb, cc, cols_c, rows_c, within_c)

    for j in range(1, nz - 1):
        kv_recv(j)
        if j + 1 < nz - 1:
            kv_send(j + 1)

    length = length_ref[0]
    real = lax.broadcasted_iota(jnp.int32, (steps, 1), 0) < length
    kv_heads = ck.shape[1] // DH
    ratio = q_ref.shape[1] // (DH * kv_heads)
    factor = DH ** (-0.5) * LOG2E
    span = math.gcd(n, 8)

    for g in range(kv_heads):
        cols = slice(g * DH, (g + 1) * DH)

        def head(j, carry):
            at = pl.ds(pl.multiple_of((g * ratio + j) * DH, DH), DH)
            q = q_ref[:, at]
            s = jnp.where(later, nt(q, ck[:, cols]), -jnp.inf)
            best = jnp.max(s, axis=1, keepdims=True)
            p = jnp.exp2((s - best) * factor)
            mass = jnp.sum(p, axis=1, keepdims=True)
            acc = nn(p.astype(BF16), cv[:, cols])

            def visit(b, part):
                best, mass, acc = part
                keys = kv[pl.ds(b * span, span), 0, :, cols].reshape(span * steps, DH)
                vals = kv[pl.ds(b * span, span), 1, :, cols].reshape(span * steps, DH)
                s = nt(q, keys)
                new = jnp.maximum(best, jnp.max(s, axis=1, keepdims=True))
                p = jnp.exp2((s - new) * factor)
                fade = jnp.exp2((best - new) * factor)
                mass = mass * fade + jnp.sum(p, axis=1, keepdims=True)
                return new, mass, acc * fade + nn(p.astype(BF16), vals)

            part = (best, mass, acc)
            if n == span:
                part = visit(0, part)
            else:
                part = lax.fori_loop(0, n // span, visit, part)
            best, mass, acc = part
            out_a[:, at] = jnp.where(real, acc / mass, 0.0).astype(BF16)
            return carry

        lax.fori_loop(0, ratio, head, 0)

    for c in range(CHUNKS):
        remote(
            x_out.at[c], state.at[(1 - y) * CHUNKS + c], x_s.at[c], x_r.at[c], other
        ).wait_recv()

    def finish(g, carry):
        lanes = pl.ds(pl.multiple_of(g * gw, gw), gw)
        off = pl.ds(pl.multiple_of(g * NS, NS), NS)
        for which, (x_ref, z_ref, c_ref, wi, gr, out) in enumerate(
            ((px, pz, pc, within_p, grow_p, out_p), (cx, cz, cc, within_c, grow_c, out_c))
        ):
            c_rows = c_ref[:, off]
            across = jnp.concatenate(
                [nn(c_rows, state[g * half_chunks + k, which]) for k in range(half_chunks)], axis=1
            )
            rows = wi[g] + across * gr[g] + skips[g, 0:1] * x_ref[:, lanes].astype(F32)
            gate = z_ref[:, lanes].astype(F32)
            gated = rows * (gate / (1.0 + jnp.exp(-gate)))
            power = jnp.sum(gated * gated, axis=1, keepdims=True) * (1.0 / gw)
            normed = gated * lax.rsqrt(power + NORM_EPS) * gain[:, lanes]
            if which == 1:
                normed = jnp.where(real, normed, 0.0)
            out[:, lanes] = normed.astype(BF16)
        return carry

    lax.fori_loop(0, groups, finish, 0)

    kv_y.wait_send()
    for c in range(CHUNKS):
        s_c[c].wait_send()
        x_c[c].wait_send()

    @pl.when(has_up)
    def _():
        for c in range(CHUNKS):
            e_c[c].wait_send()

    @pl.when(has_dn)
    def _():
        for c in range(CHUNKS):
            r_c[c].wait_send()

    for j in range(nz - 1):

        @pl.when(jnp.logical_and(has_up, z - j >= 0))
        def _():
            kv_up(j).wait_send()

        @pl.when(jnp.logical_and(has_dn, z + j < nz))
        def _():
            kv_dn(j).wait_send()


def code_decay(ref, c, value):
    value = jnp.broadcast_to(value, (8, value.shape[1]))
    high = value.astype(BF16)
    ref[c, NS : NS + 16] = jnp.concatenate([high, (value - high.astype(F32)).astype(BF16)], axis=0)


def shards(n, *args):
    args = list(args)
    args[10] = args[10].reshape(1, -1)
    args[11] = args[11].reshape(1, -1)
    px, pb, pd, pk = args[0], args[2], args[4], args[16]
    steps, hp = px.shape
    groups = pb.shape[1] // NS
    heads = pd.shape[0]
    gw = hp // groups
    per = heads // groups
    cw = hp // (2 * CHUNKS)
    nz = n // 2
    full = pl.BlockSpec(memory_space=pltpu.VMEM)
    in_specs = [full] * len(args)
    in_specs[12] = pl.BlockSpec(memory_space=pltpu.SMEM)
    dma = pltpu.SemaphoreType.DMA
    links = max(nz - 1, 1)
    scratch = [
        pltpu.VMEM((n, 2) + pk.shape, BF16),
        pltpu.VMEM((2 * CHUNKS, NS, cw), F32),
        pltpu.VMEM((2 * CHUNKS, NS + 16, cw), BF16),
        pltpu.VMEM((CHUNKS, NS + 16, cw), BF16),
        pltpu.VMEM((CHUNKS, NS, cw), F32),
        pltpu.VMEM((CHUNKS, NS, cw), BF16),
        pltpu.VMEM((CHUNKS, NS, cw), BF16),
        pltpu.VMEM((CHUNKS, NS + 16, cw), BF16),
        pltpu.VMEM((CHUNKS, NS + 16, cw), BF16),
        pltpu.VMEM((CHUNKS, 2, NS, cw), BF16),
        pltpu.VMEM((2 * CHUNKS, 2, NS, cw), BF16),
        pltpu.VMEM((CHUNKS, NS, cw), F32),
        pltpu.VMEM((groups, steps, gw), F32),
        pltpu.VMEM((groups, steps, gw), F32),
        pltpu.VMEM((groups, steps, gw), F32),
        pltpu.VMEM((groups, steps, gw), F32),
        pltpu.VMEM((groups, steps, per), F32),
        pltpu.VMEM((groups, steps, per), F32),
        pltpu.VMEM((heads, steps), F32),
        pltpu.VMEM((heads, steps), F32),
        pltpu.VMEM((groups, 8, gw), F32),
        dma,
        dma,
        dma((links,)),
        dma((links,)),
        dma((links,)),
        dma((links,)),
    ] + [dma((CHUNKS,))] * 8
    out = jax.ShapeDtypeStruct(px.shape, BF16)
    return pl.pallas_call(
        functools.partial(kernel, n),
        out_shape=(out, out, out),
        in_specs=in_specs,
        out_specs=(full, full, full),
        scratch_shapes=scratch,
        compiler_params=pltpu.CompilerParams(
            collective_id=0, has_side_effects=True, vmem_limit_bytes=56 * 2**20
        ),
    )(*args)


def solution(mesh):
    rows = P(("groups", "ctx"), "head")
    cols = P("head", ("groups", "ctx"))
    in_specs = (
        (rows,) * 4
        + (cols,)
        + (rows,) * 4
        + (cols, P("head"), P("head"), P(("groups", "ctx")))
        + (rows,) * 5
    )
    return jax.shard_map(
        functools.partial(shards, mesh.shape["ctx"]),
        mesh=mesh,
        in_specs=in_specs,
        out_specs=(rows, rows, rows),
        check_vma=False,
    )
```

time: 222 us -> 64.2 us (0.29)
  blocking collectives: 105 us -> 0 us
  Pallas kernels: 0 us -> 58.7 us
  waiting for transfers between devices: 26.2 us -> 0 us
  other arithmetic: 25.8 us -> 0 us
  local copies, waits for them, and re-layouts: 27 us -> 3.97 us
  matrix products: 20.1 us -> 0 us
  between operations: 15.8 us -> 1.3 us
    all_gather x2 -> x0, blocking collectives: 64 us -> none  [the longest x1 32.1 us: shards(): lax.all_gather(prefix_values, 'ctx', axis=0, tiled=True)]
    pallas_call x0 -> x1, Pallas kernels: none -> 58.7 us  [shards(): pl.pallas_call(functools.partial(kernel, n), out_shape=(out, out, out), i...]
    unnamed x2 -> x0, blocking collectives: 41.2 us -> none
    all_gather x1 -> x0, waiting for transfers between devices: 25.5 us -> none  [prefix(): lax.all_gather(part.astype(kind), axis)]
    dot_general x13 -> x0, matrix products: 20.1 us -> none  [the longest x2 6.69 us: visit(): jnp.einsum('qgrk,kgd->qgrd', block_weights.astype(jnp.bfloat16), block[1]...]
    select_n x16 -> x0, other arithmetic: 10.5 us -> none  [the longest x8 10.4 us: prefix_hop(): return jax.tree.map(lambda a, b: jnp.where(reached, a, b), new, before)]
    exp x8 -> x0, other arithmetic: 5.11 us -> none  [link(): jnp.exp(later[0])[..., None, None] * previous_rows[1] + later[1]]
    reshape x9 -> x0, local copies, waits for them, and re-layouts: 4.76 us -> none  [the longest x2 1.37 us: block_pieces(): c_group = c_rows.reshape(steps, groups, NS)]
  transfers between devices with their start and end apart: 2 -> 0, of which waited for: 1 -> 0; matrix products, arithmetic and copies ran while one was open for 19% -> 0% of each run, Pallas kernels for 0% -> 0%
where the time goes in v1:
time: 64.2 us; the launch traced here: 64 us
  Pallas kernels  58.7 us (91%)
  local copies, waits for them, and re-layouts  3.97 us (6%)
  between operations  1.3 us (2%)
    pallas_call x1, Pallas kernels, shards(): pl.pallas_call(functools.partial(kernel, n), out_shape=(out, out, out), i...  58.7 us
    unnamed x7, local copies, waits for them, and re-layouts  3.97 us

profile of v1, /device:TPU:0, one launch (start us, length us, event | category | flops | bytes accessed | tf_op | source)
XLA Modules:
  0.0 64.0 jit_solution(17231459408386341212)
XLA Ops:
  1.3 58.7 %shard_map.193 = (bf16[128,2048]{1,0:T(8,128)(2,1)}, bf16[128,2048]{1,0:T(8,128)(2,1)}, bf16[128,2048]{1,0:T(8,128)(2,1)}) custom-call(bf16[128,2048]{1,0:T(8,128)(2,1)} %px.1, bf16[128,2048]{1,0:T(8,128)(2,1)} %pz.1, bf16[128,512]{1,0:T(8,128)(2,1)} %pb.1, bf16[128,512]{1,0:T(8,128)(2,1)} %pc.1, f32[32,128]{1,0:T(8,128)} %pd.1, bf16[128,2048]{1,0:T(8,128)(2,1)} %cx.1, ...), custom_call_target="tpu_custom_call" | custom-call | tf_op jit(solution)/shard_map/pallas_call | solution.py:515
  60.0 0.0 copy-start.1
  60.0 1.9 %copy.25 = bf16[128,2048]{1,0:T(8,128)(2,1)} copy(bf16[128,2048]{1,0:T(8,128)(2,1)} %get-tuple-element.6) | data formatting | bytes 1048576
  62.0 0.0 copy-done.1
  62.0 0.0 copy-start
  62.0 0.8 %copy.26 = bf16[128,2048]{1,0:T(8,128)(2,1)} copy(bf16[128,2048]{1,0:T(8,128)(2,1)S(1)} %copy-done.1) | data formatting | bytes 1048576
  62.8 0.4 copy-done
  63.2 0.8 %copy.27 = bf16[128,2048]{1,0:T(8,128)(2,1)} copy(bf16[128,2048]{1,0:T(8,128)(2,1)S(1)} %copy-done) | data formatting | bytes 1048576
Async XLA Ops:
  60.0 2.0 %copy-start.1 = (bf16[128,2048]{1,0:T(8,128)(2,1)S(1)}, bf16[128,2048]{1,0:T(8,128)(2,1)}, u32[]{:S(2)}) copy-start(bf16[128,2048]{1,0:T(8,128)(2,1)} %get-tuple-element.7) | copy-start | bytes 1572868
  62.0 1.2 %copy-start = (bf16[128,2048]{1,0:T(8,128)(2,1)S(1)}, bf16[128,2048]{1,0:T(8,128)(2,1)}, u32[]{:S(2)}) copy-start(bf16[128,2048]{1,0:T(8,128)(2,1)} %get-tuple-element.8) | copy-start | bytes 1572868

commit v2 on v1

--- a/solution.py
+++ b/solution.py
@@ -11,7 +11,8 @@
 NS = 128
 DH = 128
 NORM_EPS = 1e-05
-CHUNKS = 4
+CHUNKS = 8
+LAG = 2
 LOG2E = 1.4426950408889634
 MESH = pl.DeviceIdType.MESH
 HI = lax.Precision.HIGHEST
@@ -61,9 +62,10 @@
     e_in,
     r_out,
     r_in,
-    x_out,
     state,
-    e_keep,
+    att_acc,
+    att_best,
+    att_mass,
     within_p,
     within_c,
     grow_p,
@@ -85,8 +87,6 @@
     e_r,
     r_s,
     r_r,
-    x_s,
-    x_r,
 ):
     me = lax.axis_index("ctx")
     y = lax.rem(me, 2)
@@ -124,50 +124,58 @@
             device_id_type=MESH,
         )
 
-    kv_y = remote(kv.at[me], kv.at[me], kvy_s, kvy_r, other)
-    s_c = [
-        remote(
-            s_send.at[(1 - y) * CHUNKS + c], s_in.at[c], s_s.at[c], s_r.at[c], other
-        )
-        for c in range(CHUNKS)
-    ]
+    s_c = [remote(s_send.at[c], s_in.at[c], s_s.at[c], s_r.at[c], other) for c in range(CHUNKS)]
     e_c = [remote(e_out.at[c], e_in.at[c], e_s.at[c], e_r.at[c], me + 2) for c in range(CHUNKS)]
     r_c = [remote(r_out.at[c], r_in.at[c], r_s.at[c], r_r.at[c], me - 2) for c in range(CHUNKS)]
-    x_c = [
-        remote(x_out.at[c], state.at[y * CHUNKS + c], x_s.at[c], x_r.at[c], other)
-        for c in range(CHUNKS)
-    ]
-
-    def kv_up(j):
-        at = kv.at[pl.ds(2 * (z - j), 2)]
-        return remote(at, at, up_s.at[j], up_r.at[j], me + 2)
-
-    def kv_dn(j):
-        at = kv.at[pl.ds(2 * (z + j), 2)]
-        return remote(at, at, dn_s.at[j], dn_r.at[j], me - 2)
+    links = max(nz - 1, 1)
+
+    def kv_up(at, j):
+        return remote(kv.at[y, at], kv.at[y, at], up_s.at[j], up_r.at[j], me + 2)
+
+    def kv_dn(at, j):
+        return remote(kv.at[y, at], kv.at[y, at], dn_s.at[j], dn_r.at[j], me - 2)
+
+    def kv_side(column, at, k):
+        ref = kv.at[column, at]
+        return remote(ref, ref, kvy_s.at[k], kvy_r.at[k], other)
+
+    def kv_each(j, up, down):
+        pl.when(jnp.logical_and(has_up, z - j >= 0))(lambda: up(kv_up(z - j, j)))
+        pl.when(jnp.logical_and(has_dn, z + j < nz))(lambda: down(kv_dn(z + j, j)))
 
     def kv_send(j):
-        @pl.when(jnp.logical_and(has_up, z - j >= 0))
-        def _():
-            kv_up(j).start()
-
-        @pl.when(jnp.logical_and(has_dn, z + j < nz))
-        def _():
-            kv_dn(j).start()
-
-    def kv_recv(j):
+        kv_each(j, lambda d: d.start(), lambda d: d.start())
+
+    def kv_step(j):
         @pl.when(z - 1 - j >= 0)
         def _():
-            at = kv.at[pl.ds(2 * (z - 1 - j), 2)]
-            remote(at, at, up_s.at[j], up_r.at[j], me + 2).wait_recv()
+            kv_up(z - 1 - j, j).wait_recv()
 
         @pl.when(z + 1 + j < nz)
         def _():
-            at = kv.at[pl.ds(2 * (z + 1 + j), 2)]
-            remote(at, at, dn_s.at[j], dn_r.at[j], me - 2).wait_recv()
-
-    kv[me, 0] = pk[...]
-    kv[me, 1] = pv[...]
+            kv_dn(z + 1 + j, j).wait_recv()
+
+        if j + 1 < nz - 1:
+            kv_send(j + 1)
+        kv_across(j, lambda at, k: kv_side(y, at, k).start())
+
+    def kv_across(j, act):
+        pl.when(z - 1 - j >= 0)(lambda: act(z - 1 - j, j))
+        pl.when(z + 1 + j < nz)(lambda: act(z + 1 + j, links + j))
+
+    kv[y, z, 0] = pk[...]
+    kv[y, z, 1] = pv[...]
+
+    @pl.when(jnp.logical_not(has_dn))
+    def _():
+        e_in[...] = jnp.zeros_like(e_in)
+
+    @pl.when(jnp.logical_not(has_up))
+    def _():
+        for c in range(CHUNKS):
+            r_in[c, 0:NS] = jnp.zeros((NS, cw), BF16)
+            code_decay(r_in, c, jnp.ones((1, cw), F32))
+
     t_at = lax.broadcasted_iota(jnp.int32, (steps, steps), 0)
     s_at = lax.broadcasted_iota(jnp.int32, (steps, steps), 1)
     later = t_at >= s_at
@@ -207,10 +215,11 @@
     peers = 1 + jnp.where(has_up, 1, 0) + jnp.where(has_dn, 1, 0)
     pl.semaphore_wait(barrier, peers)
 
-    s_c[0].start()
-    kv_y.start()
-    for c in range(1, CHUNKS):
+    if nz > 1:
+        kv_send(0)
+    for c in range(CHUNKS):
         s_c[c].start()
+    kv_side(y, z, 2 * links).start()
 
     lane = lax.broadcasted_iota(jnp.int32, (steps, 2 * width), 1)
 
@@ -241,175 +250,133 @@
 
     within(px, pb, pc, cols_p, rows_p, within_p)
 
-    kv_y.wait_recv()
-    kv_send(0)
+    for g in range(groups):
+        grow_c[g] = nn(jnp.exp(cols_c[g]), spread, HI)
 
     def decode(ref, c):
         return ref[c, NS : NS + 1].astype(F32) + ref[c, NS + 8 : NS + 9].astype(F32)
 
-    def own_decay(c):
-        at = y * CHUNKS + c
-        return s_send[at, NS : NS + 1].astype(F32) + s_send[at, NS + 8 : NS + 9].astype(F32)
-
     def pair_decay(c):
-        return own_decay(c) * decode(s_in, c)
-
-    for c in range(CHUNKS):
+        return decode(s_send, c) * decode(s_in, c)
+
+    def pair_sum(c):
         s_c[c].wait_recv()
-        mine = s_own[y * CHUNKS + c]
+        mine = s_own[c]
         his = s_in[c, 0:NS].astype(F32)
-        pair[c] = jnp.where(y == 0, his + decode(s_in, c) * mine, mine + own_decay(c) * his)
-
-        @pl.when(jnp.logical_not(has_dn))
-        def _():
-            e_out[c] = pair[c].astype(BF16)
-            e_keep[c] = jnp.zeros_like(e_keep[c])
+        pair[c] = jnp.where(y == 0, his + decode(s_in, c) * mine, mine + decode(s_send, c) * his)
+
+    def chain_e(c):
+        pl.when(has_dn)(lambda: e_c[c].wait_recv())
+
+        @pl.when(has_up)
+        def _():
+            e_out[c] = (pair_decay(c) * e_in[c].astype(F32) + pair[c]).astype(BF16)
             e_c[c].start()
 
-        @pl.when(jnp.logical_not(has_up))
-        def _():
-            r_out[c, 0:NS] = pair[c].astype(BF16)
-            code_decay(r_out, c, pair_decay(c))
+    def chain_r(c):
+        pl.when(has_up)(lambda: r_c[c].wait_recv())
+
+        @pl.when(has_dn)
+        def _():
+            after = decode(r_in, c)
+            r_out[c, 0:NS] = (after * pair[c] + r_in[c, 0:NS].astype(F32)).astype(BF16)
+            code_decay(r_out, c, after * pair_decay(c))
             r_c[c].start()
 
-    def chain_e(c):
-        @pl.when(has_dn)
-        def _():
-            e_c[c].wait_recv()
-            got = e_in[c].astype(F32)
-            e_keep[c] = got
-
-            @pl.when(has_up)
-            def _():
-                e_out[c] = (pair_decay(c) * got + pair[c]).astype(BF16)
-                e_c[c].start()
-
-    def chain_r(c):
-        @pl.when(has_up)
-        def _():
-            r_c[c].wait_recv()
-
-            @pl.when(has_dn)
-            def _():
-                after = decode(r_in, c)
-                r_out[c, 0:NS] = (after * pair[c] + r_in[c, 0:NS].astype(F32)).astype(BF16)
-                code_decay(r_out, c, after * pair_decay(c))
-                r_c[c].start()
-
     def settle(c):
-        at = y * CHUNKS + c
-        entry = e_keep[c]
+        entry = e_in[c].astype(F32)
         through = pair_decay(c) * entry + pair[c]
-
-        @pl.when(has_up)
-        def _():
-            x_out[c, 1] = (
-                decode(r_in, c) * through + r_in[c, 0:NS].astype(F32)
-            ).astype(BF16)
-
-        @pl.when(jnp.logical_not(has_up))
-        def _():
-            x_out[c, 1] = through.astype(BF16)
-
-        state[at, 1] = x_out[c, 1]
-        first = entry.astype(BF16)
+        state[c, 1] = (decode(r_in, c) * through + r_in[c, 0:NS].astype(F32)).astype(BF16)
 
         @pl.when(y == 0)
         def _():
-            state[at, 0] = first
-            x_out[c, 0] = (own_decay(c) * entry + s_own[at]).astype(BF16)
+            state[c, 0] = e_in[c]
 
         @pl.when(y != 0)
         def _():
-            x_out[c, 0] = first
-            state[at, 0] = (decode(s_in, c) * entry + s_in[c, 0:NS].astype(F32)).astype(BF16)
-
-        x_c[c].start()
-
-    low_half = 2 * z < nz
-
-    @pl.when(low_half)
-    def _():
-        for c in range(CHUNKS):
-            chain_e(c)
-
-    @pl.when(jnp.logical_not(low_half))
-    def _():
-        for c in range(CHUNKS):
-            chain_r(c)
-
-    if nz > 1:
-        kv_recv(0)
-        if nz > 2:
-            kv_send(1)
-
-    @pl.when(low_half)
-    def _():
-        for c in range(CHUNKS):
-            chain_r(c)
-
-    @pl.when(jnp.logical_not(low_half))
-    def _():
-        for c in range(CHUNKS):
-            chain_e(c)
-
-    for c in range(CHUNKS):
-        settle(c)
-
-    for g in range(groups):
-        grow_c[g] = nn(jnp.exp(cols_c[g]), spread, HI)
-    within(cx, cb, cc, cols_c, rows_c, within_c)
-
-    for j in range(1, nz - 1):
-        kv_recv(j)
-        if j + 1 < nz - 1:
-            kv_send(j + 1)
+            state[c, 0] = (decode(s_in, c) * entry + s_in[c, 0:NS].astype(F32)).astype(BF16)
 
     length = length_ref[0]
     real = lax.broadcasted_iota(jnp.int32, (steps, 1), 0) < length
     kv_heads = ck.shape[1] // DH
-    ratio = q_ref.shape[1] // (DH * kv_heads)
+    q_heads = q_ref.shape[1] // DH
+    ratio = q_heads // kv_heads
     factor = DH ** (-0.5) * LOG2E
-    span = math.gcd(n, 8)
-
-    for g in range(kv_heads):
-        cols = slice(g * DH, (g + 1) * DH)
-
+    span = math.gcd(nz, 8)
+
+    def seen(q, cols, column, part):
+        def visit(b, part):
+            best, mass, acc = part
+            keys = kv[column, pl.ds(b * span, span), 0, :, cols].reshape(span * steps, DH)
+            vals = kv[column, pl.ds(b * span, span), 1, :, cols].reshape(span * steps, DH)
+            s = nt(q, keys)
+            new = jnp.maximum(best, jnp.max(s, axis=1, keepdims=True))
+            p = jnp.exp2((s - new) * factor)
+            fade = jnp.exp2((best - new) * factor)
+            mass = mass * fade + jnp.sum(p, axis=1, keepdims=True)
+            return new, mass, acc * fade + nn(p.astype(BF16), vals)
+
+        if nz == span:
+            return visit(0, part)
+        return lax.fori_loop(0, nz // span, visit, part)
+
+    def attend_own(start, stop):
         def head(j, carry):
-            at = pl.ds(pl.multiple_of((g * ratio + j) * DH, DH), DH)
-            q = q_ref[:, at]
+            cols = pl.ds(pl.multiple_of(lax.div(j, ratio) * DH, DH), DH)
+            q = q_ref[:, pl.ds(pl.multiple_of(j * DH, DH), DH)]
             s = jnp.where(later, nt(q, ck[:, cols]), -jnp.inf)
             best = jnp.max(s, axis=1, keepdims=True)
             p = jnp.exp2((s - best) * factor)
             mass = jnp.sum(p, axis=1, keepdims=True)
             acc = nn(p.astype(BF16), cv[:, cols])
-
-            def visit(b, part):
-                best, mass, acc = part
-                keys = kv[pl.ds(b * span, span), 0, :, cols].reshape(span * steps, DH)
-                vals = kv[pl.ds(b * span, span), 1, :, cols].reshape(span * steps, DH)
-                s = nt(q, keys)
-                new = jnp.maximum(best, jnp.max(s, axis=1, keepdims=True))
-                p = jnp.exp2((s - new) * factor)
-                fade = jnp.exp2((best - new) * factor)
-                mass = mass * fade + jnp.sum(p, axis=1, keepdims=True)
-                return new, mass, acc * fade + nn(p.astype(BF16), vals)
-
-            part = (best, mass, acc)
-            if n == span:
-                part = visit(0, part)
-            else:
-                part = lax.fori_loop(0, n // span, visit, part)
-            best, mass, acc = part
+            att_best[j], att_mass[j], att_acc[j] = seen(q, cols, y, (best, mass, acc))
+            return carry
+
+        lax.fori_loop(start, stop, head, 0)
+
+    def attend_rest():
+        def head(j, carry):
+            cols = pl.ds(pl.multiple_of(lax.div(j, ratio) * DH, DH), DH)
+            at = pl.ds(pl.multiple_of(j * DH, DH), DH)
+            best, mass, acc = seen(
+                q_ref[:, at], cols, 1 - y, (att_best[j], att_mass[j], att_acc[j])
+            )
             out_a[:, at] = jnp.where(real, acc / mass, 0.0).astype(BF16)
             return carry
 
-        lax.fori_loop(0, ratio, head, 0)
-
-    for c in range(CHUNKS):
-        remote(
-            x_out.at[c], state.at[(1 - y) * CHUNKS + c], x_s.at[c], x_r.at[c], other
-        ).wait_recv()
+        lax.fori_loop(0, q_heads, head, 0)
+
+    low_half = 2 * z < nz
+    turns = CHUNKS + LAG
+    kv_turn = (1, 4, 6)
+    for i in range(turns):
+        if i < CHUNKS:
+            pair_sum(i)
+
+        @pl.when(low_half)
+        def _():
+            if i < CHUNKS:
+                chain_e(i)
+            if i >= LAG:
+                chain_r(i - LAG)
+
+        @pl.when(jnp.logical_not(low_half))
+        def _():
+            if i < CHUNKS:
+                chain_r(i)
+            if i >= LAG:
+                chain_e(i - LAG)
+
+        if i in kv_turn:
+            j = kv_turn.index(i)
+            for k in range(j, nz - 1 if i == kv_turn[-1] else min(j + 1, nz - 1)):
+                kv_step(k)
+        if i == 2:
+            within(cx, cb, cc, cols_c, rows_c, within_c)
+        if i >= LAG:
+            settle(i - LAG)
+        if i >= 6:
+            attend_own((i - 6) * q_heads // (turns - 6), (i - 5) * q_heads // (turns - 6))
 
     def finish(g, carry):
         lanes = pl.ds(pl.multiple_of(g * gw, gw), gw)
@@ -433,10 +400,14 @@
 
     lax.fori_loop(0, groups, finish, 0)
 
-    kv_y.wait_send()
+    kv_side(1 - y, z, 2 * links).wait_recv()
+    for j in range(nz - 1):
+        kv_across(j, lambda at, k: kv_side(1 - y, at, k).wait_recv())
+    attend_rest()
+
+    kv_side(y, z, 2 * links).wait_send()
     for c in range(CHUNKS):
         s_c[c].wait_send()
-        x_c[c].wait_send()
 
     @pl.when(has_up)
     def _():
@@ -449,14 +420,8 @@
             r_c[c].wait_send()
 
     for j in range(nz - 1):
-
-        @pl.when(jnp.logical_and(has_up, z - j >= 0))
-        def _():
-            kv_up(j).wait_send()
-
-        @pl.when(jnp.logical_and(has_dn, z + j < nz))
-        def _():
-            kv_dn(j).wait_send()
+        kv_each(j, lambda d: d.wait_send(), lambda d: d.wait_send())
+        kv_across(j, lambda at, k: kv_side(y, at, k).wait_send())
 
 
 def code_decay(ref, c, value):
@@ -475,7 +440,8 @@
     heads = pd.shape[0]
     gw = hp // groups
     per = heads // groups
-    cw = hp // (2 * CHUNKS)
+    cw = hp // CHUNKS
+    q_heads = args[13].shape[1] // DH
     nz = n // 2
     full = pl.BlockSpec(memory_space=pltpu.VMEM)
     in_specs = [full] * len(args)
@@ -483,9 +449,9 @@
     dma = pltpu.SemaphoreType.DMA
     links = max(nz - 1, 1)
     scratch = [
-        pltpu.VMEM((n, 2) + pk.shape, BF16),
-        pltpu.VMEM((2 * CHUNKS, NS, cw), F32),
-        pltpu.VMEM((2 * CHUNKS, NS + 16, cw), BF16),
+        pltpu.VMEM((2, nz, 2) + pk.shape, BF16),
+        pltpu.VMEM((CHUNKS, NS, cw), F32),
+        pltpu.VMEM((CHUNKS, NS + 16, cw), BF16),
         pltpu.VMEM((CHUNKS, NS + 16, cw), BF16),
         pltpu.VMEM((CHUNKS, NS, cw), F32),
         pltpu.VMEM((CHUNKS, NS, cw), BF16),
@@ -493,8 +459,9 @@
         pltpu.VMEM((CHUNKS, NS + 16, cw), BF16),
         pltpu.VMEM((CHUNKS, NS + 16, cw), BF16),
         pltpu.VMEM((CHUNKS, 2, NS, cw), BF16),
-        pltpu.VMEM((2 * CHUNKS, 2, NS, cw), BF16),
-        pltpu.VMEM((CHUNKS, NS, cw), F32),
+        pltpu.VMEM((q_heads, steps, DH), F32),
+        pltpu.VMEM((q_heads, steps, 1), F32),
+        pltpu.VMEM((q_heads, steps, 1), F32),
         pltpu.VMEM((groups, steps, gw), F32),
         pltpu.VMEM((groups, steps, gw), F32),
         pltpu.VMEM((groups, steps, gw), F32),
@@ -504,13 +471,13 @@
         pltpu.VMEM((heads, steps), F32),
         pltpu.VMEM((heads, steps), F32),
         pltpu.VMEM((groups, 8, gw), F32),
-        dma,
-        dma,
+        dma((2 * links + 1,)),
+        dma((2 * links + 1,)),
         dma((links,)),
         dma((links,)),
         dma((links,)),
         dma((links,)),
-    ] + [dma((CHUNKS,))] * 8
+    ] + [dma((CHUNKS,))] * 6
     out = jax.ShapeDtypeStruct(px.shape, BF16)
     return pl.pallas_call(
         functools.partial(kernel, n),

time: 64.2 us -> 88.6 us (1.38)
  Pallas kernels: 58.7 us -> 83.1 us
    pallas_call x1, Pallas kernels: 58.7 us -> 83.1 us  [shards(): pl.pallas_call(functools.partial(kernel, n), out_shape=(out, out, out), i...]
where the time goes in v2:
time: 88.6 us; the launch traced here: 88.4 us
  Pallas kernels  83.1 us (94%)
  local copies, waits for them, and re-layouts  3.97 us (4%)
  between operations  1.3 us (1%)
    pallas_call x1, Pallas kernels, shards(): pl.pallas_call(functools.partial(kernel, n), out_shape=(out, out, out), i...  83.1 us
    unnamed x7, local copies, waits for them, and re-layouts  3.97 us

profile of v2, /device:TPU:0, one launch (start us, length us, event | category | flops | bytes accessed | tf_op | source)
XLA Modules:
  0.0 88.4 jit_solution(15525053100338273159)
XLA Ops:
  1.3 83.1 %shard_map.193 = (bf16[128,2048]{1,0:T(8,128)(2,1)}, bf16[128,2048]{1,0:T(8,128)(2,1)}, bf16[128,2048]{1,0:T(8,128)(2,1)}) custom-call(bf16[128,2048]{1,0:T(8,128)(2,1)} %px.1, bf16[128,2048]{1,0:T(8,128)(2,1)} %pz.1, bf16[128,512]{1,0:T(8,128)(2,1)} %pb.1, bf16[128,512]{1,0:T(8,128)(2,1)} %pc.1, f32[32,128]{1,0:T(8,128)} %pd.1, bf16[128,2048]{1,0:T(8,128)(2,1)} %cx.1, ...), custom_call_target="tpu_custom_call" | custom-call | tf_op jit(solution)/shard_map/pallas_call | solution.py:482
  84.4 0.0 copy-start.1
  84.4 1.9 %copy.25 = bf16[128,2048]{1,0:T(8,128)(2,1)} copy(bf16[128,2048]{1,0:T(8,128)(2,1)} %get-tuple-element.6) | data formatting | bytes 1048576
  86.3 0.0 copy-done.1
  86.3 0.0 copy-start
  86.3 0.8 copy.26
  87.1 0.4 copy-done
  87.6 0.8 copy.27
Async XLA Ops:
  84.4 2.0 %copy-start.1 = (bf16[128,2048]{1,0:T(8,128)(2,1)S(1)}, bf16[128,2048]{1,0:T(8,128)(2,1)}, u32[]{:S(2)}) copy-start(bf16[128,2048]{1,0:T(8,128)(2,1)} %get-tuple-element.7) | copy-start | bytes 1572868
  86.3 1.2 %copy-start = (bf16[128,2048]{1,0:T(8,128)(2,1)S(1)}, bf16[128,2048]{1,0:T(8,128)(2,1)}, u32[]{:S(2)}) copy-start(bf16[128,2048]{1,0:T(8,128)(2,1)} %get-tuple-element.8) | copy-start | bytes 1572868

commit v3 on v1

--- a/solution.py
+++ b/solution.py
@@ -240,6 +240,9 @@
         lax.fori_loop(0, groups, group, 0)
 
     within(px, pb, pc, cols_p, rows_p, within_p)
+    for g in range(groups):
+        grow_c[g] = nn(jnp.exp(cols_c[g]), spread, HI)
+    within(cx, cb, cc, cols_c, rows_c, within_c)
 
     kv_y.wait_recv()
     kv_send(0)
@@ -347,18 +350,14 @@
     def _():
         for c in range(CHUNKS):
             chain_r(c)
+            settle(c)
 
     @pl.when(jnp.logical_not(low_half))
     def _():
         for c in range(CHUNKS):
             chain_e(c)
-
-    for c in range(CHUNKS):
-        settle(c)
-
-    for g in range(groups):
-        grow_c[g] = nn(jnp.exp(cols_c[g]), spread, HI)
-    within(cx, cb, cc, cols_c, rows_c, within_c)
+            settle(c)
+
 
     for j in range(1, nz - 1):
         kv_recv(j)

time: 64.2 us -> 64.2 us (level)
  no operation moved by 1% of the time
where the time goes in v3:
time: 64.2 us; the launch traced here: 64 us
  Pallas kernels  58.7 us (91%)
  local copies, waits for them, and re-layouts  3.97 us (6%)
  between operations  1.3 us (2%)
    pallas_call x1, Pallas kernels, shards(): pl.pallas_call(functools.partial(kernel, n), out_shape=(out, out, out), i...  58.7 us
    unnamed x7, local copies, waits for them, and re-layouts  3.97 us

profile of v3, /device:TPU:0, one launch (start us, length us, event | category | flops | bytes accessed | tf_op | source)
XLA Modules:
  0.0 64.0 jit_solution(11995253502844862978)
XLA Ops:
  1.3 58.7 %shard_map.193 = (bf16[128,2048]{1,0:T(8,128)(2,1)}, bf16[128,2048]{1,0:T(8,128)(2,1)}, bf16[128,2048]{1,0:T(8,128)(2,1)}) custom-call(bf16[128,2048]{1,0:T(8,128)(2,1)} %px.1, bf16[128,2048]{1,0:T(8,128)(2,1)} %pz.1, bf16[128,512]{1,0:T(8,128)(2,1)} %pb.1, bf16[128,512]{1,0:T(8,128)(2,1)} %pc.1, f32[32,128]{1,0:T(8,128)} %pd.1, bf16[128,2048]{1,0:T(8,128)(2,1)} %cx.1, ...), custom_call_target="tpu_custom_call" | custom-call | tf_op jit(solution)/shard_map/pallas_call | solution.py:514
  60.0 0.0 copy-start.1
  60.0 1.9 %copy.25 = bf16[128,2048]{1,0:T(8,128)(2,1)} copy(bf16[128,2048]{1,0:T(8,128)(2,1)} %get-tuple-element.6) | data formatting | bytes 1048576
  62.0 0.0 copy-done.1
  62.0 0.0 copy-start
  62.0 0.8 %copy.26 = bf16[128,2048]{1,0:T(8,128)(2,1)} copy(bf16[128,2048]{1,0:T(8,128)(2,1)S(1)} %copy-done.1) | data formatting | bytes 1048576
  62.8 0.4 copy-done
  63.2 0.8 %copy.27 = bf16[128,2048]{1,0:T(8,128)(2,1)} copy(bf16[128,2048]{1,0:T(8,128)(2,1)S(1)} %copy-done) | data formatting | bytes 1048576
Async XLA Ops:
  60.0 2.0 %copy-start.1 = (bf16[128,2048]{1,0:T(8,128)(2,1)S(1)}, bf16[128,2048]{1,0:T(8,128)(2,1)}, u32[]{:S(2)}) copy-start(bf16[128,2048]{1,0:T(8,128)(2,1)} %get-tuple-element.7) | copy-start | bytes 1572868
  62.0 1.2 %copy-start = (bf16[128,2048]{1,0:T(8,128)(2,1)S(1)}, bf16[128,2048]{1,0:T(8,128)(2,1)}, u32[]{:S(2)}) copy-start(bf16[128,2048]{1,0:T(8,128)(2,1)} %get-tuple-element.8) | copy-start | bytes 1572868
